TPU v7x, 32 devices: a whole 2x2x4 slice. The times are simulated.
32 devices in a mesh: lon: 8 (over z, y), lat: 2 (over x), tp: 2 (over core).
Axes of the slice: x: 2, y: 2, z: 4, core: 2. Of those that a mesh axis runs over, the one named last changes fastest.
Arguments:
- tokens: bfloat16 [2, 32, 256, 1024], P('tp', 'lat', 'lon'), may hold values from -6 to 6
- qkv_weight: bfloat16 [3, 1024, 1024], P(None, None, 'tp'), may hold values from -0.1875 to 0.1875
- proj_weight: bfloat16 [1024, 1024], P('tp'), may hold values from -0.1875 to 0.1875
- up_weight: bfloat16 [1024, 4096], P(None, 'tp'), may hold values from -0.1875 to 0.1875
- down_weight: bfloat16 [4096, 1024], P('tp'), may hold values from -0.09375 to 0.09375
- pos_bias: bfloat16 [16, 128, 128], P('tp'), may hold values from -400 to 400
- class_bias: bfloat16 [8, 16, 128], P(None, 'tp'), may hold values from -4 to 4
- surface_class: int32 [32, 256], P('lat', 'lon'), may hold values from 0 to 7
Outputs:
- layer_out: bfloat16 [2, 32, 256, 1024], P('tp', 'lat', 'lon')
All inputs are finite; a program needn't handle non-finite values.
Results may differ from a plain program's by a relative error of at most 0.01.
Values may be sent and summed in bfloat16 or wider, within the bound.
A program may use at most 128 MiB of HBM per device.

v0:
```python
import jax
import jax.numpy as jnp
from jax import lax
from jax.sharding import PartitionSpec as P


def padded(block, sides, width):
    for axis, dim in sides:
        count = lax.axis_size(axis)
        forward = [(i, i + 1) for i in range(count - 1)]
        forward.append((count - 1, 0))
        backward = [(target, source) for source, target in forward]
        low = lax.ppermute(
            lax.slice_in_dim(block, block.shape[dim] - width, None, axis=dim), axis, forward
        )
        high = lax.ppermute(lax.slice_in_dim(block, 0, width, axis=dim), axis, backward)
        block = jnp.concatenate([low, block, high], axis=dim)
    return block


def layer_norm(values):
    mean_value = jnp.mean(values, axis=-1, keepdims=True)
    centred = values - mean_value
    variance = jnp.mean(centred * centred, axis=-1, keepdims=True)
    return centred * lax.rsqrt(variance + 1e-05)


def to_windows(grid):
    levels, tall, broad, width = grid.shape
    split = grid.reshape(levels, tall // 8, 8, broad // 8, 8, width)
    split = jnp.transpose(split, (1, 3, 0, 2, 4, 5))
    return split.reshape(tall // 8 * (broad // 8), levels * 64, width)


def from_windows(blocks, levels, tall, broad):
    width = blocks.shape[-1]
    split = blocks.reshape(tall // 8, broad // 8, levels, 8, 8, width)
    split = jnp.transpose(split, (2, 0, 3, 1, 4, 5))
    return split.reshape(levels, tall, broad, width)


def attend(query, keys, values, bias, allowed, heads):
    count, size, width = query.shape
    head_size = width // heads
    q_four = query.reshape(count, size, heads, head_size)
    k_four = keys.reshape(count, size, heads, head_size)
    v_four = values.reshape(count, size, heads, head_size)
    scores = (
        jnp.einsum("wihc,wjhc->whij", q_four, k_four, preferred_element_type=jnp.float32)
        * head_size ** (-0.5)
        + bias
    )
    scores = jnp.where(allowed[:, None, None, :], scores, -jnp.inf)
    top = jnp.max(scores, axis=-1, keepdims=True)
    weights = jnp.exp(scores - top)
    total = jnp.sum(weights, axis=-1)
    mixed = jnp.einsum(
        "whij,wjhc->wihc", weights.astype(jnp.bfloat16), v_four, preferred_element_type=jnp.float32
    )
    mixed = mixed / jnp.transpose(total, (0, 2, 1))[..., None]
    return mixed.astype(jnp.bfloat16).reshape(count, size, width)


def project_to(grid, weight):
    return jnp.dot(grid, weight, preferred_element_type=jnp.float32).astype(jnp.bfloat16)


def body(
    tokens, qkv_weight, proj_weight, up_weight, down_weight, pos_bias, class_bias, surface_class
):
    heads = pos_bias.shape[0]
    both = lax.all_gather(tokens, "tp", axis=0, tiled=True)
    levels, tall, broad, width = both.shape
    ptall = tall + 8
    pbroad = broad + 8
    normed = layer_norm(both.astype(jnp.float32)).astype(jnp.bfloat16)
    widened = padded(normed, (("lon", 2), ("lat", 1)), 4)
    query_grid = project_to(widened, qkv_weight[0])
    key_grid = project_to(widened, qkv_weight[1])
    value_grid = project_to(widened, qkv_weight[2])
    rows_global = lax.axis_index("lat") * tall - 4 + jnp.arange(ptall, dtype=jnp.int32)
    inside = (rows_global >= 0) & (rows_global < tall * lax.axis_size("lat"))
    allowed = to_windows(jnp.broadcast_to(inside[None, :, None, None], (levels, ptall, pbroad, 1)))[
        ..., 0
    ]
    class_grid = jnp.pad(surface_class, 4)
    query_class = to_windows(
        jnp.broadcast_to(class_grid[None, :, :, None], (levels, ptall, pbroad, 1))
    )[..., 0]
    classes = class_bias.shape[0]
    one_hot = (query_class[..., None] == jnp.arange(classes, dtype=jnp.int32)).astype(jnp.float32)
    class_term = jnp.einsum(
        "wic,chj->whij", one_hot, class_bias.astype(jnp.float32), precision=lax.Precision.HIGHEST
    )
    bias = class_term + pos_bias.astype(jnp.float32)[None]
    mixed = attend(
        to_windows(query_grid), to_windows(key_grid), to_windows(value_grid), bias, allowed, heads
    )
    attended = from_windows(mixed, levels, ptall, pbroad)[:, 4 : 4 + tall, 4 : 4 + broad]
    share = lax.psum_scatter(
        jnp.dot(attended, proj_weight, preferred_element_type=jnp.float32).astype(jnp.bfloat16),
        "tp",
        scatter_dimension=0,
        tiled=True,
    ).astype(jnp.float32)
    own_hidden = (tokens.astype(jnp.float32) + share).astype(jnp.bfloat16)
    own_normed = layer_norm(own_hidden.astype(jnp.float32)).astype(jnp.bfloat16)
    normed_all = lax.all_gather(own_normed, "tp", axis=0, tiled=True)
    lifted = jnp.dot(normed_all, up_weight, preferred_element_type=jnp.float32)
    activated = jax.nn.gelu(lifted, approximate=False).astype(jnp.bfloat16)
    feed_share = lax.psum_scatter(
        jnp.dot(activated, down_weight, preferred_element_type=jnp.float32).astype(jnp.bfloat16),
        "tp",
        scatter_dimension=0,
        tiled=True,
    ).astype(jnp.float32)
    return (own_hidden.astype(jnp.float32) + feed_share).astype(jnp.bfloat16)


def solution(mesh):
    placed = (
        P("tp", "lat", "lon", None),
        P(None, None, "tp"),
        P("tp", None),
        P(None, "tp"),
        P("tp", None),
        P("tp", None, None),
        P(None, "tp", None),
        P("lat", "lon"),
    )
    return jax.shard_map(
        body, mesh=mesh, in_specs=placed, out_specs=P("tp", "lat", "lon", None), check_vma=False
    )
```

profile of v0, /device:TPU:0, one launch (start us, length us, event | category | flops | bytes accessed | tf_op | source)
XLA Modules:
  0.0 210.3 jit_solution(4867222092348660085)
XLA Ops:
  6.5 0.0 copy-start
  6.5 0.0 all-gather.3.cloned.1.call-start
  6.5 0.7 all-gather.3.cloned.1.call-update
  7.3 0.0 reduce-scatter.3.cloned.1.call-start
  7.3 14.9 %all-gather.3.cloned.1.call-done = bf16[2,16,32,1024]{3,2,1,0:T(8,128)(2,1)} async-done(((bf16[1,16,32,1024]{3,2,1,0:T(8,128)(2,1)}), bf16[2,16,32,1024]{3,2,1,0:T(8,128)(2,1)}) %all-gather.3.cloned.1.call-update) | async-done | bytes 2097168 | tf_op jit(solution)/shard_map/all_gather | solution.py:72
  22.2 1.9 convert_reduce_fusion
  24.2 2.3 %fusion.15 = f32[2,16,32]{2,1,0:T(8,128)S(1)} fusion(bf16[2,16,32,1024]{3,2,1,0:T(8,128)(2,1)} %all-gather.3.cloned.1.call-done, f32[2,16,32]{2,1,0:T(8,128)S(1)} %broadcast_multiply_fusion), kind=kLoop, calls=%fused_computation.32 | loop fusion | flops 4193280 | bytes 2105344 | tf_op jit(solution)/shard_map/reduce_sum | solution.py:24
  26.5 2.1 %fusion.16 = bf16[2,16,32,1024]{3,2,1,0:T(8,128)(2,1)S(1)} fusion(bf16[2,16,32,1024]{3,2,1,0:T(8,128)(2,1)} %all-gather.3.cloned.1.call-done, f32[2,16,32]{2,1,0:T(8,128)S(1)} %add_rsqrt_fusion, f32[2,16,32]{2,1,0:T(8,128)S(1)} %broadcast_multiply_fusion), kind=kLoop, calls=%fused_computation.33 | loop fusion | flops 4194304 | bytes 4202496 | tf_op jit(solution)/shard_map/convert_element_type | solution.py:76
  28.6 0.2 fusion.124
  28.8 1.8 collective-permute-start
  30.6 3.0 %collective-permute-start.1 = (bf16[2,16,4,1024]{3,2,1,0:T(4,128)(2,1)S(1)}, bf16[2,16,4,1024]{3,2,1,0:T(4,128)(2,1)S(1)}, u32[]{:S(2)}, u32[]{:S(2)}) collective-permute-start(bf16[2,16,4,1024]{3,2,1,0:T(4,128)(2,1)S(1)} %get-tuple-element.12), channel_id=1, source_target_pairs={{4,0},{8,4},{12,8},{16,12},{20,16},{24,20},{28,24},{0,28},{5,1},{9... | collective-permute-start | bytes 786440 | tf_op jit(solution)/shard_map/ppermute | solution.py:16
  33.6 8.7 %collective-permute-done = bf16[2,16,4,1024]{3,2,1,0:T(4,128)(2,1)S(1)} collective-permute-done((bf16[2,16,4,1024]{3,2,1,0:T(4,128)(2,1)S(1)}, bf16[2,16,4,1024]{3,2,1,0:T(4,128)(2,1)S(1)}, u32[]{:S(2)}, u32[]{:S(2)}) %collective-permute-start) | collective-permute-done | bytes 262176 | tf_op jit(solution)/shard_map/ppermute | solution.py:13
  42.3 2.2 %collective-permute-done.1 = bf16[2,16,4,1024]{3,2,1,0:T(4,128)(2,1)S(1)} collective-permute-done((bf16[2,16,4,1024]{3,2,1,0:T(4,128)(2,1)S(1)}, bf16[2,16,4,1024]{3,2,1,0:T(4,128)(2,1)S(1)}, u32[]{:S(2)}, u32[]{:S(2)}) %collective-permute-start.1) | collective-permute-done | bytes 262176 | tf_op jit(solution)/shard_map/ppermute | solution.py:16
  44.5 0.0 copy-done.7
  44.5 1.8 pad_maximum_fusion.3
  46.3 0.0 copy-done.9
  46.3 1.5 collective-permute-start.2
  47.7 0.6 collective-permute-start.3
  48.3 0.1 transpose.44
  48.4 0.1 transpose.45
  48.5 0.0 copy-done.12
  48.5 0.1 pad.4
  48.6 0.1 reshape.82
  48.7 0.1 eq.15
  48.8 0.0 copy-done.6
  48.8 0.9 copy.38
  49.8 14.5 %collective-permute-done.2 = bf16[2,4,40,1024]{3,2,1,0:T(8,128)(2,1)} collective-permute-done((bf16[2,4,40,1024]{3,2,1,0:T(8,128)(2,1)}, bf16[2,4,40,1024]{3,2,1,0:T(8,128)(2,1)}, u32[]{:S(2)}, u32[]{:S(2)}) %collective-permute-start.2) | collective-permute-done | bytes 655392 | tf_op jit(solution)/shard_map/ppermute | solution.py:13
  64.3 12.2 %collective-permute-done.3 = bf16[2,4,40,1024]{3,2,1,0:T(8,128)(2,1)} collective-permute-done((bf16[2,4,40,1024]{3,2,1,0:T(8,128)(2,1)}, bf16[2,4,40,1024]{3,2,1,0:T(8,128)(2,1)}, u32[]{:S(2)}, u32[]{:S(2)}) %collective-permute-start.3) | collective-permute-done | bytes 655392 | tf_op jit(solution)/shard_map/ppermute | solution.py:16
  76.4 4.0 %convolution_convert_fusion.2 = bf16[2,24,40,512]{3,2,1,0:T(8,128)(2,1)S(1)} fusion(bf16[3,1024,512]{2,1,0:T(8,128)(2,1)} %param.9, bf16[2,4,40,1024]{3,2,1,0:T(8,128)(2,1)} %collective-permute-done.3, bf16[2,16,4,1024]{3,2,1,0:T(4,128)(2,1)} %copy-done.9, bf16[2,16,32,1024]{3,2,1,0:T(8,128)(2,1)S(1)} %fusion.16, bf16[2,16,4,1024]{3,2,1,0:T(4,128)(2,1)} %copy-done.7, ...), kind=kOutput, calls=%fused_computation.95 | convolution fusion | flops 2033909760 | bytes 6946816 | tf_op jit(solution)/shard_map/dot_general | solution.py:65
  80.5 1.5 copy.71
  82.0 5.9 %reshape_reshape.13 = bf16[15,128,8,64]{3,2,1,0:T(8,128)(2,1)} reshape(bf16[3,5,2,8,8,512]{5,4,3,2,1,0:T(8,128)(2,1)} %bitcast.95) | data formatting | bytes 3932160 | tf_op jit(solution)/shard_map/reshape;reshape | solution.py:45
  87.9 4.0 %convolution_convert_fusion.3 = bf16[2,24,40,512]{3,2,1,0:T(8,128)(2,1)S(1)} fusion(bf16[3,1024,512]{2,1,0:T(8,128)(2,1)} %param.9, bf16[2,4,40,1024]{3,2,1,0:T(8,128)(2,1)} %collective-permute-done.3, bf16[2,16,4,1024]{3,2,1,0:T(4,128)(2,1)} %copy-done.9, bf16[2,16,32,1024]{3,2,1,0:T(8,128)(2,1)S(1)} %fusion.16, ...), kind=kOutput, calls=%fused_computation.96 | convolution fusion | flops 2033909760 | bytes 6946816 | tf_op jit(solution)/shard_map/dot_general | solution.py:65
  91.9 1.6 copy.72
  93.5 3.9 %convolution_convert_fusion.1 = bf16[2,24,40,512]{3,2,1,0:T(8,128)(2,1)S(1)} fusion(bf16[3,1024,512]{2,1,0:T(8,128)(2,1)} %param.9, bf16[2,4,40,1024]{3,2,1,0:T(8,128)(2,1)} %collective-permute-done.3, bf16[2,16,4,1024]{3,2,1,0:T(4,128)(2,1)S(1)} %copy-done.10, bf16[2,16,32,1024]{3,2,1,0:T(8,128)(2,1)S(1)} %fusion.16, ...), kind=kOutput, calls=%fused_computation.94 | convolution fusion | flops 2033909760 | bytes 6946816 | tf_op jit(solution)/shard_map/dot_general | solution.py:65
  97.4 0.0 copy-start.2
  97.4 1.5 copy.70
  98.8 5.9 %reshape_reshape.14 = bf16[15,128,8,64]{3,2,1,0:T(8,128)(2,1)} reshape(bf16[3,5,2,8,8,512]{5,4,3,2,1,0:T(8,128)(2,1)} %bitcast.96) | data formatting | bytes 3932160 | tf_op jit(solution)/shard_map/reshape;reshape | solution.py:46
  104.7 3.9 %reshape_reshape.12 = bf16[15,128,8,64]{3,2,1,0:T(8,128)(2,1)} reshape(bf16[3,5,2,8,8,512]{5,4,3,2,1,0:T(8,128)(2,1)S(1)} %bitcast.94) | data formatting | bytes 3932160 | tf_op jit(solution)/shard_map/reshape;reshape | solution.py:47
  108.6 6.2 %fusion.57 = f32[15,8,128,128]{2,3,1,0:T(8,128)S(1)} fusion(bf16[15,128,8,64]{3,2,1,0:T(8,128)(2,1)} %reshape_reshape.14, bf16[15,128,8,64]{3,2,1,0:T(8,128)(2,1)} %reshape_reshape.13), kind=kOutput, calls=%fused_computation.74 | convolution fusion | flops 251658240 | bytes 11796480 | tf_op jit(solution)/shard_map/wihc,wjhc->whij/dot_general | solution.py:49
  114.8 2.4 %fusion.125 = (f32[15,8,128]{2,1,0:T(8,128)S(1)}, f32[15,8,128,128]{2,3,1,0:T(8,128)S(1)}) fusion(f32[8,128,128]{1,2,0:T(8,128)S(1)} %copy-done.5, bf16[8,8,128]{2,1,0:T(8,128)(2,1)S(1)} %copy-done.11, s32[15,128]{1,0:T(8,128)S(1)} %eq.15, f32[15,8,128,128]{2,3,1,0:T(8,128)S(1)} %fusion.57, pred[15,128]{1,0:T(8,128)(4,1)S(1)} %transpose.45), kind=kOutput, calls=%fused_computation.154 | convolution fusion | flops 41287680 | bytes 16340352 | tf_op jit(solution)/shard_map/wic,chj->whij/dot_general | solution.py:92
  117.2 2.1 fusion.11
  119.3 0.0 copy-done.4
  119.3 1.7 fusion.55
  121.0 3.7 %copy.41 = bf16[15,128,8,64]{3,2,1,0:T(8,128)(2,1)} copy(bf16[15,128,8,64]{1,3,2,0:T(8,128)(2,1)S(1)} %fusion.55) | data formatting | bytes 3932160 | tf_op jit(solution)/shard_map/convert_element_type | solution.py:61
  124.7 5.1 %reshape_reshape.15 = bf16[3,5,2,8,8,512]{5,4,3,2,1,0:T(8,128)(2,1)S(1)} reshape(bf16[15,128,8,64]{3,2,1,0:T(8,128)(2,1)} %copy.41) | data formatting | bytes 3932160 | tf_op jit(solution)/shard_map/reshape;reshape | solution.py:37
  129.9 0.2 copy.42
  130.1 0.0 copy-start.3
  130.1 2.6 %convolution_convert_fusion = bf16[2,16,32,1024]{3,2,1,0:T(8,128)(2,1)} fusion(bf16[2,24,40,512]{3,2,1,0:T(8,128)(2,1)S(1)} %bitcast.99, bf16[512,1024]{1,0:T(8,128)(2,1)S(1)} %copy-done), kind=kOutput, calls=%fused_computation.93 | convolution fusion | flops 1074790400 | bytes 4194304 | tf_op jit(solution)/shard_map/dot_general | solution.py:101
  132.7 0.0 reduce-scatter.3.cloned.1.call-update
  132.7 0.0 all-gather.5.cloned.1.call-start
  132.8 10.5 %reduce-scatter.3.cloned.1.call-done = bf16[1,16,32,1024]{3,2,1,0:T(8,128)(2,1)} async-done(((bf16[2,16,32,1024]{3,2,1,0:T(8,128)(2,1)}), bf16[1,16,32,1024]{3,2,1,0:T(8,128)(2,1)}) %reduce-scatter.3.cloned.1.call-update) | async-done | bytes 1048592 | tf_op jit(solution)/shard_map/reduce_scatter | solution.py:100
  143.3 0.0 copy-done.3
  143.3 1.6 convert_reduce_fusion.1
  144.9 0.4 fusion.63
  145.3 1.3 fusion.64
  146.6 0.0 all-gather.5.cloned.1.call-update
  146.6 0.0 reduce-scatter.5.cloned.1.call-start
  146.7 11.9 %all-gather.5.cloned.1.call-done = bf16[2,16,32,1024]{3,2,1,0:T(8,128)(2,1)} async-done(((bf16[1,16,32,1024]{3,2,1,0:T(8,128)(2,1)}), bf16[2,16,32,1024]{3,2,1,0:T(8,128)(2,1)}) %all-gather.5.cloned.1.call-update) | async-done | bytes 2097168 | tf_op jit(solution)/shard_map/all_gather | solution.py:108
  158.5 9.0 %fusion.52 = (u16[2,32,2048]{2,1,0:T(8,128)(2,1)S(1)}, u16[2,32,2048]{2,1,0:T(8,128)(2,1)S(1)}, f32[2,16,32,2048]{3,2,1,0:T(8,128)S(1)}) fusion(bf16[2,16,32,1024]{3,2,1,0:T(8,128)(2,1)} %all-gather.5.cloned.1.call-done, bf16[1024,2048]{1,0:T(8,128)(2,1)} %param.11), kind=kOutput, calls=%fused_computation.68 | convolution fusion | flops 4321968128 | bytes 15204352 | tf_op jit(solution)/shard_map/dot_general | solution.py:109
  167.5 0.0 copy-start.1
  167.5 22.7 %fusion.68 = bf16[2,16,32,1024]{3,2,1,0:T(8,128)(2,1)} fusion(bf16[2048,1024]{1,0:T(8,128)(2,1)S(1)} %copy-done.13, f32[2,16,32,2048]{3,2,1,0:T(8,128)S(1)} %get-tuple-element.15, u16[2,32,2048]{2,1,0:T(8,128)(2,1)S(1)} %get-tuple-element.6, u16[2,32,2048]{2,1,0:T(8,128)(2,1)S(1)} %get-tuple-element.5), kind=kOutput, calls=%fused_computation.92 | convolution fusion | flops 4442816512 | bytes 15204352 | tf_op jit(solution)/shard_map/dot_general | solution.py:112
  190.3 0.0 reduce-scatter.5.cloned.1.call-update
  190.3 10.9 %reduce-scatter.5.cloned.1.call-done = bf16[1,16,32,1024]{3,2,1,0:T(8,128)(2,1)} async-done(((bf16[2,16,32,1024]{3,2,1,0:T(8,128)(2,1)}), bf16[1,16,32,1024]{3,2,1,0:T(8,128)(2,1)}) %reduce-scatter.5.cloned.1.call-update) | async-done | bytes 1048592 | tf_op jit(solution)/shard_map/reduce_scatter | solution.py:111
  201.2 2.6 %fusion.65 = bf16[1,16,32,1024]{3,2,1,0:T(8,128)(2,1)} fusion(bf16[1,16,32,1024]{3,2,1,0:T(8,128)(2,1)S(1)} %get-tuple-element.8, bf16[1,16,32,1024]{3,2,1,0:T(8,128)(2,1)} %reduce-scatter.5.cloned.1.call-done), kind=kLoop, calls=%fused_computation.85 | loop fusion | flops 2097152 | bytes 3145728 | tf_op jit(solution)/shard_map/convert_element_type | solution.py:117
  (25 shorter events, 0.1 us)
Async XLA Ops:
  6.5 123.6 %copy-start = (bf16[512,1024]{1,0:T(8,128)(2,1)S(1)}, bf16[512,1024]{1,0:T(8,128)(2,1)}, u32[]{:S(2)}) copy-start(bf16[512,1024]{1,0:T(8,128)(2,1)} %param.10) | copy-start | bytes 3145732
  6.5 42.0 %copy-start.12 = (s32[16,32]{1,0:T(8,128)S(1)}, s32[16,32]{1,0:T(8,128)}, u32[]{:S(2)}) copy-start(s32[16,32]{1,0:T(8,128)} %param.15) | copy-start | bytes 6148
  6.5 42.3 %copy-start.6 = (bf16[8,128,128]{2,1,0:T(8,128)(2,1)S(1)}, bf16[8,128,128]{2,1,0:T(8,128)(2,1)}, u32[]{:S(2)}) copy-start(bf16[8,128,128]{2,1,0:T(8,128)(2,1)} %param.13) | copy-start | bytes 786436
  6.5 15.7 %all-gather.3.cloned.1.call-start = ((), (), s32[]{:S(2)}) async-start(), calls=%async_computation.2 | async-start | bytes 3145728 | tf_op jit(solution)/shard_map/all_gather | solution.py:72
  7.3 136.0 %reduce-scatter.3.cloned.1.call-start = ((), (), s32[]{:S(2)}) async-start(), calls=%async_computation.3 | async-start | bytes 3145728 | tf_op jit(solution)/shard_map/reduce_scatter | solution.py:100
  28.8 13.4 %collective-permute-start = (bf16[2,16,4,1024]{3,2,1,0:T(4,128)(2,1)S(1)}, bf16[2,16,4,1024]{3,2,1,0:T(4,128)(2,1)S(1)}, u32[]{:S(2)}, u32[]{:S(2)}) collective-permute-start(bf16[2,16,4,1024]{3,2,1,0:T(4,128)(2,1)S(1)} %get-tuple-element.11), channel_id=1, source_target_pairs={{0,4},{4,8},{8,12},{12,16},{16,20},{20,24},{24,28},{28,0},{1,5},{5... | collective-permute-start | bytes 786440 | tf_op jit(solution)/shard_map/ppermute | solution.py:13
  30.6 13.8 %collective-permute-start.1 = (bf16[2,16,4,1024]{3,2,1,0:T(4,128)(2,1)S(1)}, bf16[2,16,4,1024]{3,2,1,0:T(4,128)(2,1)S(1)}, u32[]{:S(2)}, u32[]{:S(2)}) collective-permute-start(bf16[2,16,4,1024]{3,2,1,0:T(4,128)(2,1)S(1)} %get-tuple-element.12), channel_id=1, source_target_pairs={{4,0},{8,4},{12,8},{16,12},{20,16},{24,20},{28,24},{0,28},{5,1},{9... | collective-permute-start | bytes 786440 | tf_op jit(solution)/shard_map/ppermute | solution.py:16
  42.3 2.2 %copy-start.7 = (bf16[2,16,4,1024]{3,2,1,0:T(4,128)(2,1)}, bf16[2,16,4,1024]{3,2,1,0:T(4,128)(2,1)S(1)}, u32[]{:S(2)}) copy-start(bf16[2,16,4,1024]{3,2,1,0:T(4,128)(2,1)S(1)} %collective-permute-done) | copy-start | bytes 786436
  44.5 1.8 copy-start.9
  46.3 18.0 %collective-permute-start.2 = (bf16[2,4,40,1024]{3,2,1,0:T(8,128)(2,1)}, bf16[2,4,40,1024]{3,2,1,0:T(8,128)(2,1)}, u32[]{:S(2)}, u32[]{:S(2)}) collective-permute-start(bf16[2,4,40,1024]{3,2,1,0:T(8,128)(2,1)} %get-tuple-element.9), channel_id=1, source_target_pairs={{0,2},{2,0},{1,3},{3,1},{4,6},{6,4},{5,7},{7,5},{8,10},{10,8},{9,1... | collective-permute-start | bytes 1966088 | tf_op jit(solution)/shard_map/ppermute | solution.py:13
  47.7 28.7 %collective-permute-start.3 = (bf16[2,4,40,1024]{3,2,1,0:T(8,128)(2,1)}, bf16[2,4,40,1024]{3,2,1,0:T(8,128)(2,1)}, u32[]{:S(2)}, u32[]{:S(2)}) collective-permute-start(bf16[2,4,40,1024]{3,2,1,0:T(8,128)(2,1)} %get-tuple-element.10), channel_id=1, source_target_pairs={{2,0},{0,2},{3,1},{1,3},{6,4},{4,6},{7,5},{5,7},{10,8},{8,10},{11,... | collective-permute-start | bytes 1966088 | tf_op jit(solution)/shard_map/ppermute | solution.py:16
  80.5 7.4 %copy-start.8 = (bf16[2,16,4,1024]{3,2,1,0:T(4,128)(2,1)S(1)}, bf16[2,16,4,1024]{3,2,1,0:T(4,128)(2,1)}, u32[]{:S(2)}) copy-start(bf16[2,16,4,1024]{3,2,1,0:T(4,128)(2,1)} %copy-done.7) | copy-start | bytes 786436
  87.9 5.6 %copy-start.10 = (bf16[2,16,4,1024]{3,2,1,0:T(4,128)(2,1)S(1)}, bf16[2,16,4,1024]{3,2,1,0:T(4,128)(2,1)}, u32[]{:S(2)}) copy-start(bf16[2,16,4,1024]{3,2,1,0:T(4,128)(2,1)} %copy-done.9) | copy-start | bytes 786436
  97.4 7.4 %copy-start.2 = (bf16[2,3,8,5,8,512]{5,4,2,0,3,1:T(8,128)(2,1)S(1)}, bf16[2,3,8,5,8,512]{5,4,2,0,3,1:T(8,128)(2,1)}, u32[]{:S(2)}) copy-start(bf16[2,3,8,5,8,512]{5,4,2,0,3,1:T(8,128)(2,1)} %copy.72) | copy-start | bytes 5898244
  108.6 6.2 %copy-start.5 = (f32[8,128,128]{1,2,0:T(8,128)S(1)}, f32[8,128,128]{1,2,0:T(8,128)}, u32[]{:S(2)}) copy-start(f32[8,128,128]{1,2,0:T(8,128)} %copy.38) | copy-start | bytes 1572868
  108.6 6.2 %copy-start.11 = (bf16[8,8,128]{2,1,0:T(8,128)(2,1)S(1)}, bf16[8,8,128]{2,1,0:T(8,128)(2,1)}, u32[]{:S(2)}) copy-start(bf16[8,8,128]{2,1,0:T(8,128)(2,1)} %param.14) | copy-start | bytes 49156
  117.2 2.1 %copy-start.4 = (bf16[15,128,8,64]{3,2,1,0:T(8,128)(2,1)S(1)}, bf16[15,128,8,64]{3,2,1,0:T(8,128)(2,1)}, u32[]{:S(2)}) copy-start(bf16[15,128,8,64]{3,2,1,0:T(8,128)(2,1)} %reshape_reshape.12) | copy-start | bytes 5898244
  130.1 13.2 %copy-start.3 = (bf16[1,16,32,1024]{3,2,1,0:T(8,128)(2,1)S(1)}, bf16[1,16,32,1024]{3,2,1,0:T(8,128)(2,1)}, u32[]{:S(2)}) copy-start(bf16[1,16,32,1024]{3,2,1,0:T(8,128)(2,1)} %param.8) | copy-start | bytes 3145732
  132.7 25.8 %all-gather.5.cloned.1.call-start = ((), (), s32[]{:S(2)}) async-start(), calls=%async_computation.4 | async-start | bytes 3145728 | tf_op jit(solution)/shard_map/all_gather | solution.py:108
  146.6 54.6 %reduce-scatter.5.cloned.1.call-start = ((), (), s32[]{:S(2)}) async-start(), calls=%async_computation.5 | async-start | bytes 3145728 | tf_op jit(solution)/shard_map/reduce_scatter | solution.py:111
  158.5 9.0 %copy-start.13 = (bf16[2048,1024]{1,0:T(8,128)(2,1)S(1)}, bf16[2048,1024]{1,0:T(8,128)(2,1)}, u32[]{:S(2)}) copy-start(bf16[2048,1024]{1,0:T(8,128)(2,1)} %param.12) | copy-start | bytes 12582916
  167.5 36.3 %copy-start.1 = (bf16[512,1024]{1,0:T(8,128)(2,1)S(1)}, bf16[512,1024]{1,0:T(8,128)(2,1)}, u32[]{:S(2)}) copy-start(bf16[512,1024]{1,0:T(8,128)(2,1)} %param.10) | copy-start | bytes 3145732
Sparse Core Ops, SparseCore 0:
  8.9 13.2 all-gather.2
  132.9 10.3 reduce-scatter.2
  146.8 11.7 all-gather.4
  190.4 10.7 reduce-scatter.4
where the time goes:
time: 211 us; the launch traced here: 210 us
  waiting for transfers between devices  86.4 us (41%)
  matrix products  56.5 us (27%)
  local copies, waits for them, and re-layouts  30.9 us (15%)
  other arithmetic  16.2 us (8%)
  between operations  13.4 us (6%)
  starting transfers between devices  6.94 us (3%)
    ppermute x2, waiting for transfers between devices, padded(): lax.ppermute(lax.slice_in_dim(block, block.shape[dim] - width, None, axis...  23.2 us
    dot_general x1, matrix products, body(): jnp.dot(activated, down_weight, preferred_element_type=jnp.float32)  22.7 us
    all_gather x1, waiting for transfers between devices, body(): both = lax.all_gather(tokens, 'tp', axis=0, tiled=True)  14.9 us
    ppermute x2, waiting for transfers between devices, padded(): lax.ppermute(lax.slice_in_dim(block, 0, width, axis=dim), axis, backward)  14.4 us
    dot_general x3, matrix products, project_to(): jnp.dot(grid, weight, preferred_element_type=jnp.float32)  11.9 us
    all_gather x1, waiting for transfers between devices, body(): normed_all = lax.all_gather(own_normed, 'tp', axis=0, tiled=True)  11.9 us
    reduce_scatter x1, waiting for transfers between devices, body(): lax.psum_scatter(jnp.dot(activated, down_weight, preferred_element_type=j...  10.9 us
    reduce_scatter x1, waiting for transfers between devices, body(): lax.psum_scatter(jnp.dot(attended, proj_weight, preferred_element_type=jn...  10.5 us
  transfers between devices with their start and end apart: 8, of which 8 were waited for; matrix products, arithmetic and copies ran while one was open for 1% of the time, Pallas kernels for 0%

commit v1 on v0

v1 whole, which is shorter than its diff:
```python
import jax
import jax.numpy as jnp
from jax import lax
from jax.experimental import pallas as pl
from jax.experimental.pallas import tpu as pltpu
from jax.sharding import PartitionSpec as P

BF = jnp.bfloat16
F32 = jnp.float32


def layer_norm(values):
    mean_value = jnp.mean(values, axis=-1, keepdims=True)
    centred = values - mean_value
    variance = jnp.mean(centred * centred, axis=-1, keepdims=True)
    return centred * lax.rsqrt(variance + 1e-05)


def window_order(lat):
    new = lax.broadcasted_iota(jnp.int32, (128, 128), 0)
    old = lax.broadcasted_iota(jnp.int32, (128, 128), 1)
    half = ((new >> 6) & 1) ^ lat
    level, patch = (new >> 5) & 1, (new >> 4) & 1
    row, column = (new >> 2) & 3, new & 3
    return (old == level * 64 + half * 32 + row * 8 + patch * 4 + column).astype(BF)


def prepare_bias(lat, pos_ref, class_ref, pos_scr, class_scr):
    order = window_order(lat)
    for h in range(pos_ref.shape[0]):
        rows = jnp.dot(order, pos_ref[h], preferred_element_type=F32).astype(BF)
        pos_scr[h] = lax.dot_general(
            rows, order, (((1,), (1,)), ((), ())), preferred_element_type=F32
        )
        class_scr[h] = lax.dot_general(
            order, class_ref[h], (((1,), (1,)), ((), ())), preferred_element_type=F32
        ).astype(BF)


def scores_of(q, k, bias):
    s = lax.dot_general(q, k, (((1,), (1,)), ((), ())), preferred_element_type=F32) + bias
    return jnp.exp(s - jnp.max(s, axis=-1, keepdims=True)).astype(BF)


def attend_pair(q, k, v, hot, pos_a, pos_b, class_a, class_b):
    low_q = lax.broadcasted_iota(jnp.int32, q.shape, 1) < 64
    low_k = lax.broadcasted_iota(jnp.int32, k.shape, 1) < 64
    zero = jnp.zeros_like(v)
    one = jnp.ones_like(v)
    p_a = scores_of(jnp.where(low_q, q, hot), jnp.where(low_k, k, class_a), pos_a)
    p_b = scores_of(jnp.where(low_q, hot, q), jnp.where(low_k, class_b, k), pos_b)
    v_a = jnp.concatenate([jnp.where(low_k, v, zero), jnp.where(low_k, one, zero)], axis=1)
    v_b = jnp.concatenate([jnp.where(low_k, zero, v), jnp.where(low_k, zero, one)], axis=1)
    if k.shape[0] == 128:
        out = jnp.dot(
            jnp.concatenate([p_a, p_b], axis=1),
            jnp.concatenate([v_a, v_b], axis=0),
            preferred_element_type=F32,
        )
    else:
        out = jnp.dot(p_a, v_a, preferred_element_type=F32) + jnp.dot(
            p_b, v_b, preferred_element_type=F32
        )
    return (out[:, :128] / out[:, 128:]).astype(BF)


def attend_column(w, q_scr, k_scr, v_scr, hot_ref, pos_scr, class_scr, store):
    def rows(ref, slots, lanes):
        parts = [ref[s, w, :, lanes] for s in slots]
        return parts[0] if len(parts) == 1 else jnp.concatenate(parts, axis=0)

    everything = slice(None)
    for pair in range(q_scr.shape[-1] // 128):
        lanes = slice(pair * 128, pair * 128 + 128)
        for q_slots, k_slots, q_part, k_part in (
            ((1, 2), (1, 2), everything, everything),
            ((3,), (3, 4), slice(0, 64), everything),
            ((0,), (0,), slice(64, 128), slice(64, 128)),
        ):
            mixed = attend_pair(
                rows(q_scr, q_slots, lanes),
                rows(k_scr, k_slots, lanes),
                rows(v_scr, k_slots, lanes),
                rows(hot_ref, q_slots, everything),
                pos_scr[2 * pair, q_part, k_part],
                pos_scr[2 * pair + 1, q_part, k_part],
                class_scr[2 * pair, k_part],
                class_scr[2 * pair + 1, k_part],
            )
            for at, slot in enumerate(q_slots):
                store(slot, lanes, mixed[at * 64 : at * 64 + 64])


def attention_kernel(
    x_ref, hot_ref, w_ref, pos_ref, class_ref, out_ref, q_scr, k_scr, v_scr, pos_scr, class_scr
):
    slots, columns, tall, width = x_ref.shape
    inner = w_ref.shape[-1]
    prepare_bias(lax.axis_index("lat"), pos_ref, class_ref, pos_scr, class_scr)

    @pl.loop(0, slots)
    def _(s):
        x = x_ref[s].reshape(columns * tall, width)
        normed = layer_norm(x.astype(F32)).astype(BF)

        def project(i):
            got = jnp.dot(normed, w_ref[i], preferred_element_type=F32).astype(BF)
            return got.reshape(columns, tall, inner)

        q_scr[s] = project(0) * jnp.asarray(0.125, BF)
        k_scr[s] = project(1)
        v_scr[s] = project(2)

    @pl.loop(0, columns)
    def _(w):
        def store(slot, lanes, block):
            for level in range(2):
                for side in range(2):
                    at = level * 32 + side * 16
                    out_ref[level, slot, 2 * w + side, :, lanes] = block[at : at + 16]

        attend_column(w, q_scr, k_scr, v_scr, hot_ref, pos_scr, class_scr, store)


def feed_kernel(
    x_ref, att_ref, proj_ref, up_ref, down_ref, keep_ref, send_ref
):
    me = lax.axis_index("tp")
    rows = x_ref.shape[1]
    step = 256

    def chunk(level, at):
        here = pl.ds(pl.multiple_of(at * step, step), step)
        share = jnp.dot(
            att_ref[0, level, here], proj_ref[0], preferred_element_type=F32
        ) + jnp.dot(att_ref[1, level, here], proj_ref[1], preferred_element_type=F32)
        hidden = (x_ref[level, here].astype(F32) + share).astype(BF)
        wide = hidden.astype(F32)
        normed = layer_norm(wide).astype(BF)
        lifted = jnp.dot(normed, up_ref[...], preferred_element_type=F32)
        active = (0.5 * lifted * (1.0 + lax.erf(lifted * (0.5**0.5)))).astype(BF)
        return here, wide, jnp.dot(active, down_ref[...], preferred_element_type=F32)

    @pl.loop(0, rows // step)
    def _(at):
        here, _, part = chunk(1 - me, at)
        send_ref[here] = part.astype(BF)

    @pl.loop(0, rows // step)
    def _(at):
        here, wide, part = chunk(me, at)
        keep_ref[here] = wide + part


def around(block, axis, shift):
    count = lax.axis_size(axis)
    return lax.ppermute(block, axis, [(i, (i + shift) % count) for i in range(count)])


def whole_vmem(n):
    return [pl.BlockSpec(memory_space=pltpu.VMEM)] * n


def body(
    tokens, qkv_weight, proj_weight, up_weight, down_weight, pos_bias, class_bias, surface_class
):
    heads = pos_bias.shape[0]
    _, tall, broad, width = tokens.shape
    inner = qkv_weight.shape[-1]
    lat = lax.axis_index("lat")
    slots, patches = tall // 4, broad // 4
    columns = patches // 2 + 1

    def mirrored(grid, axis):
        return jnp.where(lat == 1, jnp.flip(grid, axis), grid)

    own = tokens.reshape(slots, 4, patches, 4, width)
    own = jnp.transpose(own, (0, 2, 1, 3, 4)).reshape(slots, patches, 16, width)
    own = mirrored(own, 0)
    both = lax.all_gather(own, "tp", axis=0, tiled=False)
    west = around(both[:, :, -1:], "lon", 1)
    east = around(both[:, :, :1], "lon", -1)
    wide = jnp.concatenate([west, both, east], axis=2)
    beyond = around(wide[:, -1:], "lat", 1)
    grid = jnp.concatenate([wide, beyond], axis=1)
    grid = grid.reshape(2, slots + 1, columns, 2, 16, width)
    grid = jnp.transpose(grid, (1, 2, 0, 3, 4, 5)).reshape(slots + 1, columns, 64, width)

    cls = jnp.pad(surface_class, ((0, 0), (4, 4))).reshape(slots, 4, columns * 2, 4)
    cls = mirrored(jnp.transpose(cls, (0, 2, 1, 3)), 0).reshape(slots, columns, 1, 2, 16)
    cls = jnp.broadcast_to(cls, (slots, columns, 2, 2, 16)).reshape(slots, columns, 64, 1)
    hot = (cls == jnp.arange(128, dtype=jnp.int32) % 64).astype(BF)
    table = jnp.transpose(class_bias, (1, 0, 2))
    classes = table.shape[1]
    table = jnp.stack(
        [
            jnp.pad(table[0::2], ((0, 0), (64, 64 - classes), (0, 0))),
            jnp.pad(table[1::2], ((0, 0), (0, 128 - classes), (0, 0))),
        ],
        axis=1,
    ).reshape(heads, 128, 128)

    attended = pl.pallas_call(
        attention_kernel,
        out_shape=jax.ShapeDtypeStruct((2, slots, 2 * columns, 16, inner), BF),
        in_specs=whole_vmem(5),
        out_specs=whole_vmem(1)[0],
        scratch_shapes=[
            pltpu.VMEM((slots + 1, columns, 64, inner), BF),
            pltpu.VMEM((slots + 1, columns, 64, inner), BF),
            pltpu.VMEM((slots + 1, columns, 64, inner), BF),
            pltpu.VMEM((heads, 128, 128), F32),
            pltpu.VMEM((heads, 128, 128), BF),
        ],
        compiler_params=pltpu.CompilerParams(vmem_limit_bytes=56 * 2**20),
        name="window_attention",
    )(grid, hot, qkv_weight, pos_bias, table)

    attended = attended[:, :, 1:-1].reshape(2, tall * broad, inner)
    attended = lax.all_gather(attended, "tp", axis=0, tiled=False)
    proj = lax.all_gather(proj_weight, "tp", axis=0, tiled=False)
    keep, send = pl.pallas_call(
        feed_kernel,
        out_shape=(
            jax.ShapeDtypeStruct((tall * broad, width), F32),
            jax.ShapeDtypeStruct((tall * broad, width), BF),
        ),
        in_specs=whole_vmem(5),
        out_specs=tuple(whole_vmem(2)),
        compiler_params=pltpu.CompilerParams(vmem_limit_bytes=56 * 2**20),
        name="project_and_feed",
    )(both.reshape(2, tall * broad, width), attended, proj, up_weight, down_weight)
    got = around(send, "tp", 1)
    out = (keep + got.astype(F32)).astype(BF).reshape(slots, patches, 4, 4, width)
    out = mirrored(out, 0)
    return jnp.transpose(out, (0, 2, 1, 3, 4)).reshape(1, tall, broad, width)


def solution(mesh):
    placed = (
        P("tp", "lat", "lon", None),
        P(None, None, "tp"),
        P("tp", None),
        P(None, "tp"),
        P("tp", None),
        P("tp", None, None),
        P(None, "tp", None),
        P("lat", "lon"),
    )
    return jax.shard_map(
        body, mesh=mesh, in_specs=placed, out_specs=P("tp", "lat", "lon", None), check_vma=False
    )
```

time: 211 us -> 134 us (0.64)
  matrix products: 56.5 us -> 0 us
  Pallas kernels: 0 us -> 45.7 us
  waiting for transfers between devices: 86.4 us -> 49.7 us
  local copies, waits for them, and re-layouts: 30.9 us -> 11.6 us
  other arithmetic: 16.2 us -> 7.44 us
    dot_general x9 -> x0, matrix products: 56.5 us -> none  [the longest x1 22.7 us: body(): jnp.dot(activated, down_weight, preferred_element_type=jnp.float32)]
    pallas_call x0 -> x2, Pallas kernels: none -> 45.7 us  [the longest x1 25.8 us: body(): pl.pallas_call(attention_kernel, out_shape=jax.ShapeDtypeStruct((2, slots...]
    reduce_scatter x2 -> x0, waiting for transfers between devices: 21.4 us -> none  [the longest x1 10.9 us: body(): lax.psum_scatter(jnp.dot(activated, down_weight, preferred_element_type=j...]
    another operation x4 -> x2, local copies, waits for them, and re-layouts: 20.8 us -> 0.82 us  [body(): jnp.stack([jnp.pad(table[0::2], ((0, 0), (64, 64 - classes), (0, 0))), jn...]
    ppermute x4, waiting for transfers between devices: 37.5 us -> 25 us  [around(): lax.ppermute(block, axis, [(i, (i + shift) % count) for i in range(count)])]
    reduce_sum x5 -> x0, other arithmetic: 8.33 us -> none  [the longest x2 3.53 us: layer_norm(): mean_value = jnp.mean(values, axis=-1, keepdims=True)]
    convert_element_type x2 -> x0, local copies, waits for them, and re-layouts: 4.64 us -> none  [the longest x1 3.71 us: attend(): return mixed.astype(jnp.bfloat16).reshape(count, size, width)]
    slice x1 -> x4, local copies, waits for them, and re-layouts: 0.21 us -> 3.39 us  [the longest x1 2.26 us: body(): attended = attended[:, :, 1:-1].reshape(2, tall * broad, inner)]
  transfers between devices with their start and end apart: 8 -> 7, of which waited for: 8 -> 6; matrix products, arithmetic and copies ran while one was open for 1% -> 8% of each run, Pallas kernels for 0% -> 19%
where the time goes in v1:
time: 134 us
  waiting for transfers between devices  49.7 us (37%)
  Pallas kernels  45.7 us (34%)
  between operations  13.3 us (10%)
  local copies, waits for them, and re-layouts  11.6 us (9%)
  other arithmetic  7.44 us (6%)
  starting transfers between devices  6.53 us (5%)
    pallas_call x1, Pallas kernels, body(): pl.pallas_call(attention_kernel, out_shape=jax.ShapeDtypeStruct((2, slots...  25.8 us
    ppermute x4, waiting for transfers between devices, around(): lax.ppermute(block, axis, [(i, (i + shift) % count) for i in range(count)])  25 us
    pallas_call x1, Pallas kernels, body(): pl.pallas_call(feed_kernel, out_shape=(jax.ShapeDtypeStruct((tall * broad...  19.9 us
    all_gather x1, waiting for transfers between devices, body(): both = lax.all_gather(own, 'tp', axis=0, tiled=False)  12.6 us
    all_gather x1, waiting for transfers between devices, body(): attended = lax.all_gather(attended, 'tp', axis=0, tiled=False)  11.3 us
    ppermute x4, starting transfers between devices, around(): lax.ppermute(block, axis, [(i, (i + shift) % count) for i in range(count)])  6.45 us
  transfers between devices with their start and end apart: 7, of which 6 were waited for; matrix products, arithmetic and copies ran while one was open for 8% of the time, Pallas kernels for 19%

profile of v1, /device:TPU:0, one launch (start us, length us, event | category | flops | bytes accessed | tf_op | source)
XLA Modules:
  0.0 134.2 jit_solution(18085872090715813376)
XLA Ops:
  6.5 0.0 all-gather.8.cloned.1.call-start
  6.5 1.5 %reshape.40 = bf16[4,4,8,4,1024]{4,3,2,1,0:T(4,128)(2,1)S(1)} reshape(bf16[1,16,32,1024]{3,2,1,0:T(8,128)(2,1)} %param.8) | data formatting | bytes 2097152 | tf_op jit(solution)/shard_map/reshape | solution.py:177
  8.0 0.6 copy.30
  8.6 0.3 reshape.41
  8.9 0.0 copy-start.1
  8.9 1.2 reverse_select_fusion.1
  10.1 0.0 all-gather.8.cloned.1.call-update
  10.2 0.0 copy-start.2
  10.2 0.0 all-gather.10.cloned.1.call-start
  10.2 0.7 all-gather.10.cloned.1.call-update
  10.9 0.0 all-gather.6.cloned.1.call-start
  11.0 12.6 %all-gather.8.cloned.1.call-done = bf16[8,8,16,1024]{3,2,1,0:T(8,128)(2,1)} async-done(((bf16[4,8,16,1024]{3,2,1,0:T(8,128)(2,1)}), bf16[8,8,16,1024]{3,2,1,0:T(8,128)(2,1)}) %all-gather.8.cloned.1.call-update) | async-done | bytes 2097168 | tf_op jit(solution)/shard_map/all_gather | solution.py:180
  23.6 1.1 fusion.1
  24.7 0.0 copy-start
  24.7 1.8 %collective-permute-start = (bf16[2,4,1,16,1024]{4,3,2,1,0:T(8,128)(2,1)S(1)}, bf16[2,4,1,16,1024]{4,3,2,1,0:T(8,128)(2,1)S(1)}, u32[]{:S(2)}, u32[]{:S(2)}) collective-permute-start(bf16[2,4,1,16,1024]{4,3,2,1,0:T(8,128)(2,1)S(1)} %get-tuple-element.9), channel_id=1, source_target_pairs={{0,4},{4,8},{8,12},{12,16},{16,20},{20,24},{24,28},{28,0},{1,5},{5... | collective-permute-start | bytes 786440 | tf_op jit(solution)/shard_map/ppermute | solution.py:157
  26.5 3.0 %collective-permute-start.1 = (bf16[2,4,1,16,1024]{4,3,2,1,0:T(8,128)(2,1)S(1)}, bf16[2,4,1,16,1024]{4,3,2,1,0:T(8,128)(2,1)S(1)}, u32[]{:S(2)}, u32[]{:S(2)}) collective-permute-start(bf16[2,4,1,16,1024]{4,3,2,1,0:T(8,128)(2,1)S(1)} %get-tuple-element.10), channel_id=1, source_target_pairs={{0,28},{4,0},{8,4},{12,8},{16,12},{20,16},{24,20},{28,24},{1,29},{... | collective-permute-start | bytes 786440 | tf_op jit(solution)/shard_map/ppermute | solution.py:157
  29.4 0.0 copy-done.1
  29.5 0.1 pad_bitcast_fusion
  29.6 8.5 %collective-permute-done = bf16[2,4,1,16,1024]{4,3,2,1,0:T(8,128)(2,1)S(1)} collective-permute-done((bf16[2,4,1,16,1024]{4,3,2,1,0:T(8,128)(2,1)S(1)}, bf16[2,4,1,16,1024]{4,3,2,1,0:T(8,128)(2,1)S(1)}, u32[]{:S(2)}, u32[]{:S(2)}) %collective-permute-start) | collective-permute-done | bytes 262176 | tf_op jit(solution)/shard_map/ppermute | solution.py:157
  38.1 2.2 %collective-permute-done.1 = bf16[2,4,1,16,1024]{4,3,2,1,0:T(8,128)(2,1)S(1)} collective-permute-done((bf16[2,4,1,16,1024]{4,3,2,1,0:T(8,128)(2,1)S(1)}, bf16[2,4,1,16,1024]{4,3,2,1,0:T(8,128)(2,1)S(1)}, u32[]{:S(2)}, u32[]{:S(2)}) %collective-permute-start.1) | collective-permute-done | bytes 262176 | tf_op jit(solution)/shard_map/ppermute | solution.py:157
  40.3 2.0 %pad_maximum_fusion.1 = bf16[2,1,10,16,1024]{4,3,2,1,0:T(8,128)(2,1)} fusion(bf16[2,4,1,16,1024]{4,3,2,1,0:T(8,128)(2,1)S(1)} %collective-permute-done.1, bf16[2,4,8,16,1024]{4,3,2,1,0:T(8,128)(2,1)} %bitcast.28, bf16[2,4,1,16,1024]{4,3,2,1,0:T(8,128)(2,1)S(1)} %collective-permute-done), kind=kLoop, calls=%fused_computation.6 | loop fusion | flops 655360 | bytes 3276800 | tf_op jit(solution)/shard_map/concatenate | solution.py:183
  42.3 1.5 %collective-permute-start.2 = (bf16[2,1,10,16,1024]{4,3,2,1,0:T(8,128)(2,1)}, bf16[2,1,10,16,1024]{4,3,2,1,0:T(8,128)(2,1)S(1)}, u32[]{:S(2)}, u32[]{:S(2)}) collective-permute-start(bf16[2,1,10,16,1024]{4,3,2,1,0:T(8,128)(2,1)} %pad_maximum_fusion.1), channel_id=1, source_target_pairs={{0,2},{2,0},{1,3},{3,1},{4,6},{6,4},{5,7},{7,5},{8,10},{10,8},{9,1... | collective-permute-start | bytes 1966088 | tf_op jit(solution)/shard_map/ppermute | solution.py:157
  43.7 0.2 pad_maximum_fusion.3
  43.9 0.8 copy.26
  44.7 0.0 copy-done.2
  44.7 0.1 copy.28
  44.8 0.1 reshape.45
  44.9 0.1 rev.13
  45.0 0.4 copy.23
  45.4 0.1 broadcast_in_dim.8
  45.5 0.1 eq.23
  45.6 1.0 compare_convert_fusion.hot_ref
  46.6 11.6 %collective-permute-done.2 = bf16[2,1,10,16,1024]{4,3,2,1,0:T(8,128)(2,1)S(1)} collective-permute-done((bf16[2,1,10,16,1024]{4,3,2,1,0:T(8,128)(2,1)}, bf16[2,1,10,16,1024]{4,3,2,1,0:T(8,128)(2,1)S(1)}, u32[]{:S(2)}, u32[]{:S(2)}) %collective-permute-start.2) | collective-permute-done | bytes 655392 | tf_op jit(solution)/shard_map/ppermute | solution.py:157
  58.3 0.0 copy-done
  58.3 0.5 pad_maximum_fusion
  58.8 2.1 %copy.21 = bf16[5,5,2,2,16,1024]{5,4,3,2,1,0:T(8,128)(2,1)} copy(bf16[5,5,2,2,16,1024]{5,4,3,1,0,2:T(8,128)(2,1)S(1)} %bitcast.31) | data formatting | bytes 6553600 | tf_op jit(solution)/shard_map/transpose | solution.py:187
  60.9 25.8 %window_attention.1 = bf16[2,4,10,16,512]{4,3,2,1,0:T(8,128)(2,1)} custom-call(bf16[5,5,64,1024]{3,2,1,0:T(8,128)(2,1)} %bitcast.32, bf16[4,5,64,128]{3,2,1,0:T(8,128)(2,1)} %compare_convert_fusion.hot_ref, bf16[3,1024,512]{2,1,0:T(8,128)(2,1)} %w_ref.1, bf16[8,128,128]{2,1,0:T(8,128)(2,1)} %pos_ref.1, bf16[8,128,128]{2,1,0:T(8,128)(2,1)} %bitcast.36), custom_call_target="tpu_custom_call" | custom-call | tf_op jit(solution)/shard_map/window_attention/pallas_call | solution.py:203
  86.7 2.3 %slice.26 = bf16[2,4,8,16,512]{4,3,2,1,0:T(8,128)(2,1)} slice(bf16[2,4,10,16,512]{4,3,2,1,0:T(8,128)(2,1)} %window_attention.1), slice={[0:2], [0:4], [1:9], [0:16], [0:512]} | slice | bytes 2097152 | tf_op jit(solution)/shard_map/slice | solution.py:219
  89.0 0.0 all-gather.6.cloned.1.call-update
  89.0 0.0 all-gather.10.cloned.1.call-done
  89.0 11.3 %all-gather.6.cloned.1.call-done.att_ref = bf16[2,2,512,512]{3,2,1,0:T(8,128)(2,1)} async-done(((bf16[1,2,512,512]{3,2,1,0:T(8,128)(2,1)}), bf16[2,2,512,512]{3,2,1,0:T(8,128)(2,1)}) %all-gather.6.cloned.1.call-update) | async-done | bytes 2097168 | tf_op jit(solution)/shard_map/all_gather | solution.py:220
  100.3 19.9 %project_and_feed.1 = (f32[512,1024]{1,0:T(8,128)}, bf16[512,1024]{1,0:T(8,128)(2,1)}) custom-call(bf16[2,512,1024]{2,1,0:T(8,128)(2,1)} %bitcast.29, bf16[2,2,512,512]{3,2,1,0:T(8,128)(2,1)} %all-gather.6.cloned.1.call-done.att_ref, bf16[2,512,1024]{2,1,0:T(8,128)(2,1)} %bitcast.35, bf16[1024,2048]{1,0:T(8,128)(2,1)} %up_ref.1, bf16[2048,1024]{1,0:T(8,128)(2,1)} %down_ref.1), custom_call_target="tpu_custom_call" | custom-call | tf_op jit(solution)/shard_map/project_and_feed/pallas_call | solution.py:222
  120.2 0.2 collective-permute-start.3
  120.4 2.7 %collective-permute-done.3 = bf16[512,1024]{1,0:T(8,128)(2,1)S(1)} collective-permute-done((bf16[512,1024]{1,0:T(8,128)(2,1)}, bf16[512,1024]{1,0:T(8,128)(2,1)S(1)}, u32[]{:S(2)}, u32[]{:S(2)}) %collective-permute-start.3) | collective-permute-done | bytes 1048608 | tf_op jit(solution)/shard_map/ppermute | solution.py:157
  123.1 2.0 %add_convert_fusion = bf16[512,1024]{1,0:T(8,128)(2,1)S(1)} fusion(f32[512,1024]{1,0:T(8,128)} %get-tuple-element.7, bf16[512,1024]{1,0:T(8,128)(2,1)S(1)} %collective-permute-done.3), kind=kLoop, calls=%fused_computation.1 | loop fusion | flops 1572864 | bytes 4194304 | tf_op jit(solution)/shard_map/convert_element_type | solution.py:234
  125.1 0.4 reshape.47
  125.5 0.5 fusion
  126.0 0.5 copy.27
  126.5 1.1 reshape.48
  (8 shorter events, 0.1 us)
Async XLA Ops:
  6.5 17.1 %all-gather.8.cloned.1.call-start = ((), (), s32[]{:S(2)}) async-start(), calls=%async_computation.1 | async-start | bytes 3145728 | tf_op jit(solution)/shard_map/all_gather | solution.py:180
  8.9 20.6 %copy-start.1 = (bf16[8,8,128]{2,1,0:T(8,128)(2,1)S(1)}, bf16[8,8,128]{2,1,0:T(8,128)(2,1)}, u32[]{:S(2)}) copy-start(bf16[8,8,128]{2,1,0:T(8,128)(2,1)} %param.14) | copy-start | bytes 49156
  10.2 34.5 %copy-start.2 = (s32[16,32]{1,0:T(8,128)S(1)}, s32[16,32]{1,0:T(8,128)}, u32[]{:S(2)}) copy-start(s32[16,32]{1,0:T(8,128)} %param.15) | copy-start | bytes 6148
  10.2 78.8 %all-gather.10.cloned.1.call-start = ((), (), s32[]{:S(2)}) async-start(), calls=%async_computation.2 | async-start | bytes 3145728 | tf_op jit(solution)/shard_map/all_gather | solution.py:221
  10.9 89.3 %all-gather.6.cloned.1.call-start = ((), (), s32[]{:S(2)}) async-start(), calls=%async_computation | async-start | bytes 3145728 | tf_op jit(solution)/shard_map/all_gather | solution.py:220
  24.7 33.6 %copy-start = (bf16[8,8,16,1024]{3,2,1,0:T(8,128)(2,1)S(1)}, bf16[8,8,16,1024]{3,2,1,0:T(8,128)(2,1)}, u32[]{:S(2)}) copy-start(bf16[8,8,16,1024]{3,2,1,0:T(8,128)(2,1)} %all-gather.8.cloned.1.call-done) | copy-start | bytes 6291460
  24.7 13.4 %collective-permute-start = (bf16[2,4,1,16,1024]{4,3,2,1,0:T(8,128)(2,1)S(1)}, bf16[2,4,1,16,1024]{4,3,2,1,0:T(8,128)(2,1)S(1)}, u32[]{:S(2)}, u32[]{:S(2)}) collective-permute-start(bf16[2,4,1,16,1024]{4,3,2,1,0:T(8,128)(2,1)S(1)} %get-tuple-element.9), channel_id=1, source_target_pairs={{0,4},{4,8},{8,12},{12,16},{16,20},{20,24},{24,28},{28,0},{1,5},{5... | collective-permute-start | bytes 786440 | tf_op jit(solution)/shard_map/ppermute | solution.py:157
  26.5 13.8 %collective-permute-start.1 = (bf16[2,4,1,16,1024]{4,3,2,1,0:T(8,128)(2,1)S(1)}, bf16[2,4,1,16,1024]{4,3,2,1,0:T(8,128)(2,1)S(1)}, u32[]{:S(2)}, u32[]{:S(2)}) collective-permute-start(bf16[2,4,1,16,1024]{4,3,2,1,0:T(8,128)(2,1)S(1)} %get-tuple-element.10), channel_id=1, source_target_pairs={{0,28},{4,0},{8,4},{12,8},{16,12},{20,16},{24,20},{28,24},{1,29},{... | collective-permute-start | bytes 786440 | tf_op jit(solution)/shard_map/ppermute | solution.py:157
  42.3 16.0 %collective-permute-start.2 = (bf16[2,1,10,16,1024]{4,3,2,1,0:T(8,128)(2,1)}, bf16[2,1,10,16,1024]{4,3,2,1,0:T(8,128)(2,1)S(1)}, u32[]{:S(2)}, u32[]{:S(2)}) collective-permute-start(bf16[2,1,10,16,1024]{4,3,2,1,0:T(8,128)(2,1)} %pad_maximum_fusion.1), channel_id=1, source_target_pairs={{0,2},{2,0},{1,3},{3,1},{4,6},{6,4},{5,7},{7,5},{8,10},{10,8},{9,1... | collective-permute-start | bytes 1966088 | tf_op jit(solution)/shard_map/ppermute | solution.py:157
  120.2 2.9 %collective-permute-start.3 = (bf16[512,1024]{1,0:T(8,128)(2,1)}, bf16[512,1024]{1,0:T(8,128)(2,1)S(1)}, u32[]{:S(2)}, u32[]{:S(2)}) collective-permute-start(bf16[512,1024]{1,0:T(8,128)(2,1)} %get-tuple-element.8), channel_id=1, source_target_pairs={{0,1},{1,0},{2,3},{3,2},{4,5},{5,4},{6,7},{7,6},{8,9},{9,8},{10,11... | collective-permute-start | bytes 3145736 | tf_op jit(solution)/shard_map/ppermute | solution.py:157
Sparse Core Ops, SparseCore 0:
  10.3 13.2 all-gather.7
  25.1 11.7 all-gather.9
  89.1 11.1 all-gather.5

commit v2 on v0

v2 whole, which is shorter than its diff:
```python
import jax
import jax.numpy as jnp
from jax import lax
from jax.experimental import pallas as pl
from jax.experimental.pallas import tpu as pltpu
from jax.sharding import PartitionSpec as P

BF = jnp.bfloat16
F32 = jnp.float32


def layer_norm(values):
    mean_value = jnp.mean(values, axis=-1, keepdims=True)
    centred = values - mean_value
    variance = jnp.mean(centred * centred, axis=-1, keepdims=True)
    return centred * lax.rsqrt(variance + 1e-05)


def window_order(lat):
    new = lax.broadcasted_iota(jnp.int32, (128, 128), 0)
    old = lax.broadcasted_iota(jnp.int32, (128, 128), 1)
    half = ((new >> 6) & 1) ^ lat
    level, patch = (new >> 5) & 1, (new >> 4) & 1
    row, column = (new >> 2) & 3, new & 3
    return (old == level * 64 + half * 32 + row * 8 + patch * 4 + column).astype(BF)


def prepare_bias(lat, pos_ref, class_ref, pos_scr, class_scr):
    order = window_order(lat)
    classes = class_ref.shape[1]
    for h in range(pos_ref.shape[0]):
        rows = jnp.dot(order, pos_ref[h], preferred_element_type=F32).astype(BF)
        pos_scr[h] = lax.dot_general(
            rows, order, (((1,), (1,)), ((), ())), preferred_element_type=F32
        )
        ahead = 64 if h % 2 == 0 else 0
        parts = [class_ref[h], jnp.zeros((128 - ahead - classes, 128), F32)]
        if ahead:
            parts = [jnp.zeros((ahead, 128), F32)] + parts
        table = jnp.concatenate(parts, axis=0).astype(BF)
        class_scr[h] = lax.dot_general(
            order, table, (((1,), (1,)), ((), ())), preferred_element_type=F32
        ).astype(BF)


def scores_of(q, k, bias):
    s = lax.dot_general(q, k, (((1,), (1,)), ((), ())), preferred_element_type=F32) + bias
    return jnp.exp(s - jnp.max(s, axis=-1, keepdims=True)).astype(BF)


def attend_pair(q, k, v, hot, pos_a, pos_b, class_a, class_b):
    low_q = lax.broadcasted_iota(jnp.int32, q.shape, 1) < 64
    low_k = lax.broadcasted_iota(jnp.int32, k.shape, 1) < 64
    zero = jnp.zeros_like(v)
    one = jnp.ones_like(v)
    p_a = scores_of(jnp.where(low_q, q, hot), jnp.where(low_k, k, class_a), pos_a)
    p_b = scores_of(jnp.where(low_q, hot, q), jnp.where(low_k, class_b, k), pos_b)
    v_a = jnp.concatenate([jnp.where(low_k, v, zero), jnp.where(low_k, one, zero)], axis=1)
    v_b = jnp.concatenate([jnp.where(low_k, zero, v), jnp.where(low_k, zero, one)], axis=1)
    if k.shape[0] == 128:
        out = jnp.dot(
            jnp.concatenate([p_a, p_b], axis=1),
            jnp.concatenate([v_a, v_b], axis=0),
            preferred_element_type=F32,
        )
    else:
        out = jnp.dot(p_a, v_a, preferred_element_type=F32) + jnp.dot(
            p_b, v_b, preferred_element_type=F32
        )
    return (out[:, :128] / out[:, 128:]).astype(BF)


def band_order(broad):
    size = 4 * broad
    new = lax.broadcasted_iota(jnp.int32, (size, size), 0)
    old = lax.broadcasted_iota(jnp.int32, (size, size), 1)
    return (old == ((new // 4) % 4) * broad + (new // 16) * 4 + new % 4).astype(BF)


WINDOWS = (
    ((1, 2), (1, 2), slice(None), slice(None)),
    ((0,), (0,), slice(64, 128), slice(64, 128)),
    ((3,), (3, 4), slice(0, 64), slice(None)),
)


def layer_kernel(
    tok_ref, cell_ref, pos_ref, class_ref, qkv_hbm, proj_hbm, up_hbm, down_hbm, out_ref,
    x, q_scr, k_scr, v_scr, hot, pos_scr, class_scr, att, keep, send, recv,
    qkv_ref, proj_ref, up_ref, down_ref, local_sem, send_sem, recv_sem,
):
    bands, size, width = tok_ref.shape
    patches = size // 16
    inner = att.shape[-1]
    lon, lat, me = lax.axis_index("lon"), lax.axis_index("lat"), lax.axis_index("tp")
    lons = lax.axis_size("lon")
    other, across = 1 - me, 1 - lat
    east, west = lax.rem(lon + 1, lons), lax.rem(lon + lons - 1, lons)
    peer = (lon, lat, other)

    loads = [pltpu.make_async_copy(qkv_hbm.at[i], qkv_ref.at[i], local_sem.at[i]) for i in range(3)]
    loads += [
        pltpu.make_async_copy(proj_hbm, proj_ref.at[me], local_sem.at[3]),
        pltpu.make_async_copy(up_hbm, up_ref, local_sem.at[4]),
        pltpu.make_async_copy(down_hbm, down_ref, local_sem.at[5]),
    ]
    for load in loads:
        load.start()

    friends = [peer]
    for core in (me, other):
        friends += [(east, lat, core), (west, lat, core), (lon, across, core)]
        friends += [(east, across, core), (west, across, core)]
    barrier = pltpu.get_barrier_semaphore()
    for friend in friends:
        pl.semaphore_signal(
            barrier, inc=1, device_id=friend, device_id_type=pl.DeviceIdType.MESH
        )

    order = band_order(size // 4)

    @pl.loop(0, bands)
    def _(s):
        row = jnp.where(lat == 1, bands - 1 - s, s)
        moved = jnp.dot(order, tok_ref[row], preferred_element_type=F32).astype(BF)
        x[me, s, 1 : patches + 1] = moved.reshape(patches, 16, width)

    pl.semaphore_wait(barrier, len(friends))
    count = 0

    def remote(source, target, device):
        nonlocal count
        copy = pltpu.make_async_remote_copy(
            src_ref=source,
            dst_ref=target,
            send_sem=send_sem.at[count],
            recv_sem=recv_sem.at[count],
            device_id=device,
            device_id_type=pl.DeviceIdType.MESH,
        )
        count += 1
        return copy

    mine = x.at[me, 0:bands, 1 : patches + 1]
    twin = [remote(mine, mine, peer)]
    sides, beyond = [], []
    for core in (me, other):
        sides.append(remote(x.at[me, 0:bands, patches], x.at[me, 0:bands, 0], (east, lat, core)))
        sides.append(remote(x.at[me, 0:bands, 1], x.at[me, 0:bands, patches + 1], (west, lat, core)))
    for core in (me, other):
        inside = slice(1, patches + 1)
        beyond.append(
            remote(x.at[me, bands - 1, inside], x.at[me, bands, inside], (lon, across, core))
        )
        beyond.append(
            remote(x.at[me, bands - 1, patches], x.at[me, bands, 0], (east, across, core))
        )
        beyond.append(
            remote(x.at[me, bands - 1, 1], x.at[me, bands, patches + 1], (west, across, core))
        )
    projs = [remote(proj_hbm, proj_ref.at[me], peer)]
    for copy in twin + sides + beyond + projs:
        copy.start()

    prepare_bias(lat, pos_ref, class_ref, pos_scr, class_scr)

    @pl.loop(0, bands)
    def _(s):
        row = jnp.where(lat == 1, bands - 1 - s, s)
        lane = lax.broadcasted_iota(jnp.int32, (128, size), 0) % 64
        flags = (lane == cell_ref[row]).astype(F32).astype(BF)
        block = lax.dot_general(
            order, flags, (((1,), (1,)), ((), ())), preferred_element_type=F32
        ).astype(BF)
        for level in range(2):
            hot[s, level, 1 : patches + 1] = block.reshape(patches, 16, 128)

    def normal(rows):
        return layer_norm(rows.astype(F32)).astype(BF)

    def project(normed, i):
        return jnp.dot(normed, qkv_ref[i], preferred_element_type=F32).astype(BF)

    def project_level(level):
        @pl.loop(0, bands)
        def _(s):
            normed = normal(x[level, s, 1 : patches + 1].reshape(size, width))
            for i, ref in enumerate((q_scr, k_scr, v_scr)):
                got = project(normed, i)
                if i == 0:
                    got = got * jnp.asarray(0.125, BF)
                ref[s, level, 1 : patches + 1] = got.reshape(patches, 16, inner)

    for load in loads[:3]:
        load.wait()
    project_level(me)
    twin[0].wait_recv()
    project_level(other)
    for copy in sides:
        copy.wait_recv()

    @pl.loop(0, 2)
    def _(level):
        half = bands * 16
        rows = jnp.concatenate(
            [
                x[level, 0:bands, 0].reshape(half, width),
                x[level, 0:bands, patches + 1].reshape(half, width),
            ],
            axis=0,
        )
        normed = normal(rows)
        for i, ref in ((1, k_scr), (2, v_scr)):
            got = project(normed, i)
            ref[0:bands, level, 0] = got[:half].reshape(bands, 16, inner)
            ref[0:bands, level, patches + 1] = got[half:].reshape(bands, 16, inner)

    def attend_windows(windows):
        @pl.loop(0, patches // 2 + 1)
        def _(w):
            def rows(ref, slots, lanes):
                parts = [ref[s, :, pl.ds(2 * w, 2), :, lanes].reshape(64, 128) for s in slots]
                return parts[0] if len(parts) == 1 else jnp.concatenate(parts, axis=0)

            for pair in range(inner // 128):
                lanes = slice(pair * 128, pair * 128 + 128)
                for q_slots, k_slots, q_part, k_part in windows:
                    mixed = attend_pair(
                        rows(q_scr, q_slots, lanes),
                        rows(k_scr, k_slots, lanes),
                        rows(v_scr, k_slots, lanes),
                        rows(hot, q_slots, slice(None)),
                        pos_scr[2 * pair, q_part, k_part],
                        pos_scr[2 * pair + 1, q_part, k_part],
                        class_scr[2 * pair, k_part],
                        class_scr[2 * pair + 1, k_part],
                    )
                    for at, slot in enumerate(q_slots):
                        block = mixed[at * 64 : at * 64 + 64].reshape(2, 2, 16, 128)
                        att[me, slot, :, pl.ds(2 * w, 2), :, lanes] = block

    def share(first, last):
        part = att.at[me, first:last, :, 1 : patches + 1]
        copy = remote(part, part, peer)
        copy.start()
        return copy

    attend_windows(WINDOWS[:2])
    early = share(0, bands - 1)
    for copy in beyond:
        copy.wait_recv()

    @pl.loop(0, 2)
    def _(level):
        normed = normal(x[level, bands].reshape(size + 32, width))
        for i, ref in ((1, k_scr), (2, v_scr)):
            ref[bands, level] = project(normed, i).reshape(patches + 2, 16, inner)

    attend_windows(WINDOWS[2:])
    late = share(bands - 1, bands)
    for load in loads[3:]:
        load.wait()
    projs[0].wait_recv()
    early.wait_recv()
    pieces = 4
    hidden_units = up_ref.shape[1] // pieces

    def feed(level, at):
        slots = pl.ds(2 * at, 2)
        wide = x[level, slots, 1 : patches + 1].reshape(2 * size, width).astype(F32)
        for half in range(2):
            mixed = att[half, slots, level, 1 : patches + 1].reshape(2 * size, inner)
            if half == 0:
                total = jnp.dot(mixed, proj_ref[half], preferred_element_type=F32)
            else:
                total += jnp.dot(mixed, proj_ref[half], preferred_element_type=F32)
        wide = (wide + total).astype(BF).astype(F32)
        normed = normal(wide)
        total = None
        for piece in range(pieces):
            units = slice(piece * hidden_units, (piece + 1) * hidden_units)
            lifted = jnp.dot(normed, up_ref[:, units], preferred_element_type=F32)
            active = (0.5 * lifted * (1.0 + lax.erf(lifted * (0.5**0.5)))).astype(BF)
            part = jnp.dot(active, down_ref[units], preferred_element_type=F32)
            total = part if total is None else total + part
        return wide, total

    steps = bands // 2
    returns = [remote(send.at[at], recv.at[at], peer) for at in range(steps)]
    for at in range(steps):
        if at == steps - 1:
            late.wait_recv()
        _, total = feed(other, at)
        send[at] = total.astype(BF)
        returns[at].start()

    @pl.loop(0, steps)
    def _(at):
        wide, total = feed(me, at)
        keep[at] = wide + total

    for at in range(steps):
        returns[at].wait_recv()
    back = band_order(size // 4)

    @pl.loop(0, bands)
    def _(s):
        row = jnp.where(lat == 1, bands - 1 - s, s)
        at, here = s // 2, pl.ds((s % 2) * size, size)
        done = (keep[at, here] + recv[at, here].astype(F32)).astype(BF)
        out_ref[row] = lax.dot_general(
            back, done, (((0,), (0,)), ((), ())), preferred_element_type=F32
        ).astype(BF)

    for copy in twin + sides + beyond + projs + [early, late] + returns:
        copy.wait_send()


def body(
    tokens, qkv_weight, proj_weight, up_weight, down_weight, pos_bias, class_bias, surface_class
):
    heads = pos_bias.shape[0]
    _, tall, broad, width = tokens.shape
    inner, units = qkv_weight.shape[-1], up_weight.shape[-1]
    bands, patches, size = tall // 4, broad // 4, 4 * broad
    copies = 1 + 4 + 6 + 1 + 2 + bands // 2
    vmem = pl.BlockSpec(memory_space=pltpu.VMEM)
    anywhere = pl.BlockSpec(memory_space=pl.ANY)
    scratch = (
        ((2, bands + 1, patches + 2, 16, width), BF),
        ((bands, 2, patches + 2, 16, inner), BF),
        ((bands + 1, 2, patches + 2, 16, inner), BF),
        ((bands + 1, 2, patches + 2, 16, inner), BF),
        ((bands, 2, patches + 2, 16, 128), BF),
        ((heads, 128, 128), F32),
        ((heads, 128, 128), BF),
        ((2, bands, 2, patches + 2, 16, inner), BF),
        ((bands // 2, 2 * size, width), F32),
        ((bands // 2, 2 * size, width), BF),
        ((bands // 2, 2 * size, width), BF),
        (qkv_weight.shape, BF),
        ((2,) + proj_weight.shape, BF),
        (up_weight.shape, BF),
        (down_weight.shape, BF),
    )
    out = pl.pallas_call(
        layer_kernel,
        out_shape=jax.ShapeDtypeStruct((bands, size, width), BF),
        in_specs=[vmem] * 4 + [anywhere] * 4,
        out_specs=vmem,
        scratch_shapes=[pltpu.VMEM(shape, kind) for shape, kind in scratch]
        + [
            pltpu.SemaphoreType.DMA((6,)),
            pltpu.SemaphoreType.DMA((copies,)),
            pltpu.SemaphoreType.DMA((copies,)),
        ],
        compiler_params=pltpu.CompilerParams(
            collective_id=0, has_side_effects=True, vmem_limit_bytes=58 * 2**20
        ),
        cost_estimate=pl.CostEstimate(
            flops=17 * 10**9, bytes_accessed=16 * 2**20, transcendentals=4 * 10**6
        ),
        name="window_layer",
    )(
        tokens.reshape(bands, size, width),
        surface_class.reshape(bands, 1, size),
        pos_bias,
        jnp.transpose(class_bias, (1, 0, 2)).astype(F32),
        qkv_weight,
        proj_weight,
        up_weight,
        down_weight,
    )
    return out.reshape(1, tall, broad, width)


def solution(mesh):
    placed = (
        P("tp", "lat", "lon", None),
        P(None, None, "tp"),
        P("tp", None),
        P(None, "tp"),
        P("tp", None),
        P("tp", None, None),
        P(None, "tp", None),
        P("lat", "lon"),
    )
    return jax.shard_map(
        body, mesh=mesh, in_specs=placed, out_specs=P("tp", "lat", "lon", None), check_vma=False
    )
```

time: 211 us -> 58.9 us (0.28)
  waiting for transfers between devices: 86.4 us -> 0 us
  matrix products: 56.5 us -> 0 us
  Pallas kernels: 0 us -> 53.1 us
  local copies, waits for them, and re-layouts: 30.9 us -> 3.65 us
  other arithmetic: 16.2 us -> 1.33 us
  between operations: 13.4 us -> 0.01 us
  starting transfers between devices: 6.94 us -> 0 us
    dot_general x9 -> x0, matrix products: 56.5 us -> none  [the longest x1 22.7 us: body(): jnp.dot(activated, down_weight, preferred_element_type=jnp.float32)]
    pallas_call x0 -> x1, Pallas kernels: none -> 53.1 us  [body(): pl.pallas_call(layer_kernel, out_shape=jax.ShapeDtypeStruct((bands, size,...]
    ppermute x4 -> x0, waiting for transfers between devices: 37.5 us -> none  [the longest x2 23.2 us: padded(): lax.ppermute(lax.slice_in_dim(block, block.shape[dim] - width, None, axis...]
    all_gather x2 -> x0, waiting for transfers between devices: 26.8 us -> none  [the longest x1 14.9 us: body(): both = lax.all_gather(tokens, 'tp', axis=0, tiled=True)]
    reduce_scatter x2 -> x0, waiting for transfers between devices: 21.4 us -> none  [the longest x1 10.9 us: body(): lax.psum_scatter(jnp.dot(activated, down_weight, preferred_element_type=j...]
    another operation x4 -> x0, local copies, waits for them, and re-layouts: 20.8 us -> none  [the longest x1 5.87 us: attend(): k_four = keys.reshape(count, size, heads, head_size)]
    reduce_sum x5 -> x0, other arithmetic: 8.33 us -> none  [the longest x2 3.53 us: layer_norm(): mean_value = jnp.mean(values, axis=-1, keepdims=True)]
    ppermute x4 -> x0, starting transfers between devices: 6.82 us -> none  [the longest x2 3.56 us: padded(): lax.ppermute(lax.slice_in_dim(block, 0, width, axis=dim), axis, backward)]
  transfers between devices with their start and end apart: 8 -> 0, of which waited for: 8 -> 0; matrix products, arithmetic and copies ran while one was open for 1% -> 0% of each run, Pallas kernels for 0% -> 0%
where the time goes in v2:
time: 58.9 us; the launch traced here: 58.1 us
  Pallas kernels  53.1 us (90%)
  local copies, waits for them, and re-layouts  3.65 us (6%)
  other arithmetic  1.33 us (2%)
    pallas_call x1, Pallas kernels, body(): pl.pallas_call(layer_kernel, out_shape=jax.ShapeDtypeStruct((bands, size,...  53.1 us
    unnamed x1, local copies, waits for them, and re-layouts  2.29 us
    reshape x1, local copies, waits for them, and re-layouts, body(): surface_class.reshape(bands, 1, size)  1.36 us
    convert_element_type x1, other arithmetic, body(): jnp.transpose(class_bias, (1, 0, 2)).astype(F32)  1.33 us

profile of v2, /device:TPU:0, one launch (start us, length us, event | category | flops | bytes accessed | tf_op | source)
XLA Modules:
  0.0 58.1 jit_solution(13719641238333565385)
XLA Ops:
  0.0 1.4 %reshape.10.cell_ref = s32[4,1,128]{2,1,0:T(1,128)} reshape(s32[16,32]{1,0:T(8,128)} %param.15) | data formatting | bytes 4096 | tf_op jit(solution)/shard_map/reshape | solution.py:366
  1.4 1.3 %convert_bitcast_fusion.class_ref = f32[8,8,128]{2,1,0:T(8,128)} fusion(bf16[8,8,128]{2,1,0:T(8,128)(2,1)} %param.14), kind=kLoop, calls=%fused_computation | loop fusion | flops 8192 | bytes 49152 | tf_op jit(solution)/shard_map/convert_element_type | solution.py:368
  2.7 53.1 %window_layer.1 = bf16[4,128,1024]{2,1,0:T(8,128)(2,1)} custom-call(bf16[4,128,1024]{2,1,0:T(8,128)(2,1)} %bitcast.5, s32[4,1,128]{2,1,0:T(1,128)} %reshape.10.cell_ref, bf16[8,128,128]{2,1,0:T(8,128)(2,1)} %pos_ref.1, f32[8,8,128]{2,1,0:T(8,128)} %convert_bitcast_fusion.class_ref, bf16[3,1024,512]{2,1,0:T(8,128)(2,1)} %qkv_hbm.1, ...), custom_call_target="tpu_custom_call" | custom-call | flops 16999999488 | bytes 16777216 | tf_op jit(solution)/shard_map/window_layer/pallas_call | solution.py:346
  55.8 2.3 %copy.12 = bf16[1,16,32,1024]{3,2,1,0:T(8,128)(2,1)} copy(bf16[1,16,32,1024]{3,2,1,0:T(8,128)(2,1)} %bitcast.4) | data formatting | bytes 2097152

commit v3 on v2

--- a/solution.py
+++ b/solution.py
@@ -27,20 +27,21 @@
 
 def prepare_bias(lat, pos_ref, class_ref, pos_scr, class_scr):
     order = window_order(lat)
-    classes = class_ref.shape[1]
-    for h in range(pos_ref.shape[0]):
+    classes, heads, keys = class_ref.shape
+    flat = class_ref[...].astype(F32).reshape(classes * heads, keys).astype(BF)
+    flat = lax.dot_general(
+        order, flat, (((1,), (1,)), ((), ())), preferred_element_type=F32
+    ).astype(BF)
+    entry = lax.broadcasted_iota(jnp.int32, (classes * heads, 128), 0)
+    lane = lax.broadcasted_iota(jnp.int32, (classes * heads, 128), 1)
+    for h in range(heads):
         rows = jnp.dot(order, pos_ref[h], preferred_element_type=F32).astype(BF)
         pos_scr[h] = lax.dot_general(
             rows, order, (((1,), (1,)), ((), ())), preferred_element_type=F32
         )
         ahead = 64 if h % 2 == 0 else 0
-        parts = [class_ref[h], jnp.zeros((128 - ahead - classes, 128), F32)]
-        if ahead:
-            parts = [jnp.zeros((ahead, 128), F32)] + parts
-        table = jnp.concatenate(parts, axis=0).astype(BF)
-        class_scr[h] = lax.dot_general(
-            order, table, (((1,), (1,)), ((), ())), preferred_element_type=F32
-        ).astype(BF)
+        pick = (entry == (lane - ahead) * heads + h).astype(F32).astype(BF)
+        class_scr[h] = jnp.dot(flat, pick, preferred_element_type=F32).astype(BF)
 
 
 def scores_of(q, k, bias):
@@ -168,7 +169,8 @@
     def _(s):
         row = jnp.where(lat == 1, bands - 1 - s, s)
         lane = lax.broadcasted_iota(jnp.int32, (128, size), 0) % 64
-        flags = (lane == cell_ref[row]).astype(F32).astype(BF)
+        cells = jnp.concatenate([cell_ref[pl.ds(4 * row + i, 1)] for i in range(4)], axis=1)
+        flags = (lane == cells).astype(F32).astype(BF)
         block = lax.dot_general(
             order, flags, (((1,), (1,)), ((), ())), preferred_element_type=F32
         ).astype(BF)
@@ -182,42 +184,24 @@
         return jnp.dot(normed, qkv_ref[i], preferred_element_type=F32).astype(BF)
 
     def project_level(level):
-        @pl.loop(0, bands)
-        def _(s):
-            normed = normal(x[level, s, 1 : patches + 1].reshape(size, width))
-            for i, ref in enumerate((q_scr, k_scr, v_scr)):
-                got = project(normed, i)
-                if i == 0:
-                    got = got * jnp.asarray(0.125, BF)
-                ref[s, level, 1 : patches + 1] = got.reshape(patches, 16, inner)
+        inside = slice(1, patches + 1)
+        normed = normal(x[level, 0:bands, inside].reshape(bands * size, width))
+        for i, ref in enumerate((q_scr, k_scr, v_scr)):
+            got = project(normed, i)
+            if i == 0:
+                got = got * jnp.asarray(0.125, BF)
+            ref[0:bands, level, inside] = got.reshape(bands, patches, 16, inner)
 
     for load in loads[:3]:
         load.wait()
     project_level(me)
     twin[0].wait_recv()
     project_level(other)
-    for copy in sides:
-        copy.wait_recv()
-
-    @pl.loop(0, 2)
-    def _(level):
-        half = bands * 16
-        rows = jnp.concatenate(
-            [
-                x[level, 0:bands, 0].reshape(half, width),
-                x[level, 0:bands, patches + 1].reshape(half, width),
-            ],
-            axis=0,
-        )
-        normed = normal(rows)
-        for i, ref in ((1, k_scr), (2, v_scr)):
-            got = project(normed, i)
-            ref[0:bands, level, 0] = got[:half].reshape(bands, 16, inner)
-            ref[0:bands, level, patches + 1] = got[half:].reshape(bands, 16, inner)
-
-    def attend_windows(windows):
-        @pl.loop(0, patches // 2 + 1)
-        def _(w):
+    def attend_windows(windows, places, first, stride):
+        @pl.loop(0, places)
+        def _(i):
+            w = first + i * stride
+
             def rows(ref, slots, lanes):
                 parts = [ref[s, :, pl.ds(2 * w, 2), :, lanes].reshape(64, 128) for s in slots]
                 return parts[0] if len(parts) == 1 else jnp.concatenate(parts, axis=0)
@@ -245,31 +229,44 @@
         copy.start()
         return copy
 
-    attend_windows(WINDOWS[:2])
+    attend_windows(WINDOWS[:2], patches // 2 - 1, 1, 1)
+    for copy in sides:
+        copy.wait_recv()
+
+    half = bands * 16
+    ends = [(level, place) for level in range(2) for place in (0, patches + 1)]
+    rows = [x[level, 0:bands, place].reshape(half, width) for level, place in ends]
+    normed = normal(jnp.concatenate(rows, axis=0))
+    for i, ref in ((1, k_scr), (2, v_scr)):
+        got = project(normed, i)
+        for at, (level, place) in enumerate(ends):
+            part = got[at * half : at * half + half]
+            ref[0:bands, level, place] = part.reshape(bands, 16, inner)
+
+    attend_windows(WINDOWS[:2], 2, 0, patches // 2)
     early = share(0, bands - 1)
     for copy in beyond:
         copy.wait_recv()
 
-    @pl.loop(0, 2)
-    def _(level):
-        normed = normal(x[level, bands].reshape(size + 32, width))
-        for i, ref in ((1, k_scr), (2, v_scr)):
-            ref[bands, level] = project(normed, i).reshape(patches + 2, 16, inner)
-
-    attend_windows(WINDOWS[2:])
+    normed = normal(x[:, bands].reshape(2 * (size + 32), width))
+    for i, ref in ((1, k_scr), (2, v_scr)):
+        ref[bands] = project(normed, i).reshape(2, patches + 2, 16, inner)
+
+    attend_windows(WINDOWS[2:], patches // 2 + 1, 0, 1)
     late = share(bands - 1, bands)
     for load in loads[3:]:
         load.wait()
     projs[0].wait_recv()
     early.wait_recv()
     pieces = 4
+    group = send.shape[1] // size
     hidden_units = up_ref.shape[1] // pieces
 
     def feed(level, at):
-        slots = pl.ds(2 * at, 2)
-        wide = x[level, slots, 1 : patches + 1].reshape(2 * size, width).astype(F32)
+        slots = slice(group * at, group * at + group)
+        wide = x[level, slots, 1 : patches + 1].reshape(group * size, width).astype(F32)
         for half in range(2):
-            mixed = att[half, slots, level, 1 : patches + 1].reshape(2 * size, inner)
+            mixed = att[half, slots, level, 1 : patches + 1].reshape(group * size, inner)
             if half == 0:
                 total = jnp.dot(mixed, proj_ref[half], preferred_element_type=F32)
             else:
@@ -285,7 +282,7 @@
             total = part if total is None else total + part
         return wide, total
 
-    steps = bands // 2
+    steps = bands // group
     returns = [remote(send.at[at], recv.at[at], peer) for at in range(steps)]
     for at in range(steps):
         if at == steps - 1:
@@ -294,23 +291,19 @@
         send[at] = total.astype(BF)
         returns[at].start()
 
-    @pl.loop(0, steps)
-    def _(at):
+    back = band_order(size // 4)
+    for at in range(steps):
         wide, total = feed(me, at)
-        keep[at] = wide + total
-
-    for at in range(steps):
+        keep[...] = wide + total
         returns[at].wait_recv()
-    back = band_order(size // 4)
-
-    @pl.loop(0, bands)
-    def _(s):
-        row = jnp.where(lat == 1, bands - 1 - s, s)
-        at, here = s // 2, pl.ds((s % 2) * size, size)
-        done = (keep[at, here] + recv[at, here].astype(F32)).astype(BF)
-        out_ref[row] = lax.dot_general(
-            back, done, (((0,), (0,)), ((), ())), preferred_element_type=F32
-        ).astype(BF)
+        for part in range(group):
+            s = at * group + part
+            row = jnp.where(lat == 1, bands - 1 - s, s)
+            here = slice(part * size, (part + 1) * size)
+            done = (keep[here] + recv[at, here].astype(F32)).astype(BF)
+            out_ref[row] = lax.dot_general(
+                back, done, (((0,), (0,)), ((), ())), preferred_element_type=F32
+            ).astype(BF)
 
     for copy in twin + sides + beyond + projs + [early, late] + returns:
         copy.wait_send()
@@ -323,7 +316,8 @@
     _, tall, broad, width = tokens.shape
     inner, units = qkv_weight.shape[-1], up_weight.shape[-1]
     bands, patches, size = tall // 4, broad // 4, 4 * broad
-    copies = 1 + 4 + 6 + 1 + 2 + bands // 2
+    group = 4
+    copies = 1 + 4 + 6 + 1 + 2 + bands // group
     vmem = pl.BlockSpec(memory_space=pltpu.VMEM)
     anywhere = pl.BlockSpec(memory_space=pl.ANY)
     scratch = (
@@ -335,9 +329,9 @@
         ((heads, 128, 128), F32),
         ((heads, 128, 128), BF),
         ((2, bands, 2, patches + 2, 16, inner), BF),
-        ((bands // 2, 2 * size, width), F32),
-        ((bands // 2, 2 * size, width), BF),
-        ((bands // 2, 2 * size, width), BF),
+        ((group * size, width), F32),
+        ((bands // group, group * size, width), BF),
+        ((bands // group, group * size, width), BF),
         (qkv_weight.shape, BF),
         ((2,) + proj_weight.shape, BF),
         (up_weight.shape, BF),
@@ -363,9 +357,9 @@
         name="window_layer",
     )(
         tokens.reshape(bands, size, width),
-        surface_class.reshape(bands, 1, size),
+        surface_class,
         pos_bias,
-        jnp.transpose(class_bias, (1, 0, 2)).astype(F32),
+        class_bias,
         qkv_weight,
         proj_weight,
         up_weight,

time: 58.9 us -> 49.9 us (0.85); the launches traced: 58.1 us -> 49.7 us
  Pallas kernels: 53.1 us -> 47.4 us
  local copies, waits for them, and re-layouts: 3.65 us -> 2.29 us
  other arithmetic: 1.33 us -> 0 us
    pallas_call x1, Pallas kernels: 53.1 us -> 47.4 us  [body(): pl.pallas_call(layer_kernel, out_shape=jax.ShapeDtypeStruct((bands, size,...]
    reshape x1 -> x0, local copies, waits for them, and re-layouts: 1.36 us -> none  [body(): surface_class.reshape(bands, 1, size)]
    convert_element_type x1 -> x0, other arithmetic: 1.33 us -> none  [body(): jnp.transpose(class_bias, (1, 0, 2)).astype(F32)]
where the time goes in v3:
time: 49.9 us; the launch traced here: 49.7 us
  Pallas kernels  47.4 us (95%)
  local copies, waits for them, and re-layouts  2.29 us (5%)
    pallas_call x1, Pallas kernels, body(): pl.pallas_call(layer_kernel, out_shape=jax.ShapeDtypeStruct((bands, size,...  47.4 us
    unnamed x1, local copies, waits for them, and re-layouts  2.29 us

profile of v3, /device:TPU:0, one launch (start us, length us, event | category | flops | bytes accessed | tf_op | source)
XLA Modules:
  0.0 49.7 jit_solution(5838720118604859198)
XLA Ops:
  0.0 47.4 %window_layer.1 = bf16[4,128,1024]{2,1,0:T(8,128)(2,1)} custom-call(bf16[4,128,1024]{2,1,0:T(8,128)(2,1)} %bitcast.3, s32[16,32]{1,0:T(8,128)} %cell_ref.1, bf16[8,128,128]{2,1,0:T(8,128)(2,1)} %pos_ref.1, bf16[8,8,128]{2,1,0:T(8,128)(2,1)} %class_ref.1, bf16[3,1024,512]{2,1,0:T(8,128)(2,1)} %qkv_hbm.1, bf16[512,1024]{1,0:T(8,128)(2,1)} %proj_hbm.1, ...), custom_call_target="tpu_custom_call" | custom-call | flops 16999999488 | bytes 16777216 | tf_op jit(solution)/shard_map/window_layer/pallas_call | solution.py:340
  47.4 2.3 %copy.10 = bf16[1,16,32,1024]{3,2,1,0:T(8,128)(2,1)} copy(bf16[1,16,32,1024]{3,2,1,0:T(8,128)(2,1)} %bitcast.2) | data formatting | bytes 2097152

commit v4 on v3

--- a/solution.py
+++ b/solution.py
@@ -258,7 +258,7 @@
         load.wait()
     projs[0].wait_recv()
     early.wait_recv()
-    pieces = 4
+    pieces = 2
     group = send.shape[1] // size
     hidden_units = up_ref.shape[1] // pieces
 

time: 49.9 us -> 49.7 us (level)
  no operation moved by 1% of the time
where the time goes in v4:
time: 49.7 us; the launch traced here: 49.5 us
  Pallas kernels  47.2 us (95%)
  local copies, waits for them, and re-layouts  2.29 us (5%)
    pallas_call x1, Pallas kernels, body(): pl.pallas_call(layer_kernel, out_shape=jax.ShapeDtypeStruct((bands, size,...  47.2 us
    unnamed x1, local copies, waits for them, and re-layouts  2.29 us

profile of v4, /device:TPU:0, one launch (start us, length us, event | category | flops | bytes accessed | tf_op | source)
XLA Modules:
  0.0 49.5 jit_solution(1474595985005157438)
XLA Ops:
  0.0 47.2 %window_layer.1 = bf16[4,128,1024]{2,1,0:T(8,128)(2,1)} custom-call(bf16[4,128,1024]{2,1,0:T(8,128)(2,1)} %bitcast.3, s32[16,32]{1,0:T(8,128)} %cell_ref.1, bf16[8,128,128]{2,1,0:T(8,128)(2,1)} %pos_ref.1, bf16[8,8,128]{2,1,0:T(8,128)(2,1)} %class_ref.1, bf16[3,1024,512]{2,1,0:T(8,128)(2,1)} %qkv_hbm.1, bf16[512,1024]{1,0:T(8,128)(2,1)} %proj_hbm.1, ...), custom_call_target="tpu_custom_call" | custom-call | flops 16999999488 | bytes 16777216 | tf_op jit(solution)/shard_map/window_layer/pallas_call | solution.py:340
  47.2 2.3 %copy.10 = bf16[1,16,32,1024]{3,2,1,0:T(8,128)(2,1)} copy(bf16[1,16,32,1024]{3,2,1,0:T(8,128)(2,1)} %bitcast.2) | data formatting | bytes 2097152
